TPU v7x, 32 devices: a whole 2x2x4 slice. The times are simulated.
32 devices in a mesh: row: 4 (over y, x), col: 8 (over z, core).
Axes of the slice: x: 2, y: 2, z: 4, core: 2. Of those that a mesh axis runs over, the one named last changes fastest.
Arguments:
- precond: float32 [8, 8192, 8192], P(None, 'row', 'col'), may hold values from -6 to 6
- out_factors: bfloat16 [1536, 8192], P('col', 'row'), may hold values from -6 to 6
- in_factors: bfloat16 [1536, 8192], P('row', 'col'), may hold values from -6 to 6
- token_mask: int32 [1536], replicated, may hold values 0 or 1
- seq_ids: int32 [1536], replicated, may hold values from 0 to 3, never falling along the last dimension, each value on 1 to 576 neighbouring positions
- query_ids: int32 [8], replicated, may hold values from 0 to 7, each once
Outputs:
- scores: float32 [8, 4], replicated
Inputs may be any that keep to these rules, and one draw needn't show every extreme that they name: seq_ids never falls along the tokens; each sequence has 1 to 576 tokens. query_ids names each query once.
All inputs are finite; a program needn't handle non-finite values.
Results may differ from a plain program's by a relative error of at most 0.0003.
Values may be sent and summed in bfloat16 or wider, within the bound.
A program may use at most 128 MiB of HBM per device.

v0:
```python
import math

import jax
import jax.numpy as jnp
from jax import lax
from jax.sharding import PartitionSpec as P

DOUT = 8192
DIN = 8192
SEQ = 4
LEN = 384


def shards(precond, out_factors, in_factors, token_mask, seq_ids, query_ids):
    num_queries = precond.shape[0]
    weight = token_mask.astype(jnp.float32)[:, None] * (
        seq_ids[:, None] == jnp.arange(SEQ, dtype=jnp.int32)[None, :]
    ).astype(jnp.float32)
    out_whole = lax.all_gather(out_factors, "col", axis=0, tiled=True)
    out_wide = out_whole.astype(jnp.float32)
    in_wide = lax.all_gather(in_factors, "row", axis=0, tiled=True).astype(jnp.float32)

    def one_query(query_grad):
        mapped = lax.dot_general(
            in_wide, query_grad, (((1,), (1,)), ((), ())), precision=lax.Precision.HIGHEST
        )
        per_token = jnp.sum(mapped * out_wide, axis=1)
        return jnp.dot(per_token, weight, precision=lax.Precision.HIGHEST)

    total = lax.map(one_query, precond)
    summed = lax.psum(total, ("row", "col"))
    select = (query_ids[:, None] == jnp.arange(num_queries, dtype=jnp.int32)[None, :]).astype(
        jnp.float32
    )
    scale = 1.0 / math.sqrt(DOUT * DIN * LEN)
    return jnp.dot(select, summed, precision=lax.Precision.HIGHEST) * scale


def solution(mesh):
    placed = (P(None, "row", "col"), P("col", "row"), P("row", "col"), P(), P(), P())
    return jax.shard_map(shards, mesh=mesh, in_specs=placed, out_specs=P(), check_vma=False)
```

profile of v0, /device:TPU:0, one launch (start us, length us, event | category | flops | bytes accessed | tf_op | source)
XLA Modules:
  0.0 541.8 jit_solution(918385708753429817)
XLA Ops:
  6.5 0.0 all-gather.3.cloned.1.call-start
  6.5 0.7 all-gather.3.cloned.1.call-update
  7.3 0.0 all-gather.5.cloned.1.call-start
  7.3 0.7 all-gather.5.cloned.1.call-update
  8.0 0.7 convert_element_type.13
  8.7 47.2 %all-gather.3.cloned.1.call-done = bf16[1536,1024]{1,0:T(8,128)(2,1)} async-done(((bf16[384,1024]{1,0:T(8,128)(2,1)}), bf16[1536,1024]{1,0:T(8,128)(2,1)}) %all-gather.3.cloned.1.call-update) | async-done | bytes 3145744 | tf_op jit(solution)/shard_map/all_gather | solution.py:21
  55.9 5.2 convert_element_type.11
  61.1 0.0 copy-start
  61.1 61.2 %all-gather.5.cloned.1.call-done = bf16[1536,2048]{1,0:T(8,128)(2,1)} async-done(((bf16[192,2048]{1,0:T(8,128)(2,1)}), bf16[1536,2048]{1,0:T(8,128)(2,1)}) %all-gather.5.cloned.1.call-update) | async-done | bytes 6291472 | tf_op jit(solution)/shard_map/all_gather | solution.py:19
  122.3 8.9 %convert_element_type.12 = f32[1536,2048]{1,0:T(8,128)} convert(bf16[1536,2048]{1,0:T(8,128)(2,1)} %all-gather.5.cloned.1.call-done) | non-fusion elementwise | flops 3145728 | bytes 18874368 | tf_op jit(solution)/shard_map/convert_element_type | solution.py:20
  131.2 0.0 copy-done
  131.2 0.0 copy-start.1
  131.2 364.1 %while.11 = (s32[]{:T(128)}, f32[8,4]{1,0:T(8,128)S(1)}, f32[8,2048,1024]{2,1,0:T(8,128)}, f32[1536,1024]{1,0:T(8,128)}, f32[1536,2048]{1,0:T(8,128)}, /*index=5...) while((s32[]{:T(128)}, f32[8,4]{1,0:T(8,128)S(1)}, f32[8,2048,1024]{2,1,0:T(8,128)}, ...), condition=%wide.region_2.3_spmd.clone, body=%wide.region_0.2_spmd.clone.sunk | while | flops 38661083136 | bytes 27300496 | solution.py:30
  131.2 44.6 %fusion.26 = f32[1536]{0:T(1024)S(1)} fusion(f32[1536,2048]{1,0:T(8,128)} %get-tuple-element.135, f32[1536,1024]{1,0:T(8,128)} %get-tuple-element.134, f32[8,2048,1024]{2,1,0:T(8,128)} %get-tuple-element.133, s32[]{:T(128)} %get-tuple-element.122), kind=kOutput, calls=%fused_computation.2.clone.1 | convolution fusion | flops 38660997120 | bytes 27269632 | tf_op jit(solution)/shard_map/while/body/eval_jaxpr/dot_general | solution.py:24
  175.8 0.8 fusion.27
  176.7 44.6 %fusion.26 = f32[1536]{0:T(1024)S(1)} fusion(f32[1536,2048]{1,0:T(8,128)} %get-tuple-element.135, f32[1536,1024]{1,0:T(8,128)} %get-tuple-element.134, f32[8,2048,1024]{2,1,0:T(8,128)} %get-tuple-element.133, s32[]{:T(128)} %get-tuple-element.122), kind=kOutput, calls=%fused_computation.2.clone.1 | convolution fusion | flops 38660997120 | bytes 27269632 | tf_op jit(solution)/shard_map/while/body/eval_jaxpr/dot_general | solution.py:24
  221.3 0.8 fusion.27
  222.2 44.6 %fusion.26 = f32[1536]{0:T(1024)S(1)} fusion(f32[1536,2048]{1,0:T(8,128)} %get-tuple-element.135, f32[1536,1024]{1,0:T(8,128)} %get-tuple-element.134, f32[8,2048,1024]{2,1,0:T(8,128)} %get-tuple-element.133, s32[]{:T(128)} %get-tuple-element.122), kind=kOutput, calls=%fused_computation.2.clone.1 | convolution fusion | flops 38660997120 | bytes 27269632 | tf_op jit(solution)/shard_map/while/body/eval_jaxpr/dot_general | solution.py:24
  266.8 0.8 fusion.27
  267.7 44.6 %fusion.26 = f32[1536]{0:T(1024)S(1)} fusion(f32[1536,2048]{1,0:T(8,128)} %get-tuple-element.135, f32[1536,1024]{1,0:T(8,128)} %get-tuple-element.134, f32[8,2048,1024]{2,1,0:T(8,128)} %get-tuple-element.133, s32[]{:T(128)} %get-tuple-element.122), kind=kOutput, calls=%fused_computation.2.clone.1 | convolution fusion | flops 38660997120 | bytes 27269632 | tf_op jit(solution)/shard_map/while/body/eval_jaxpr/dot_general | solution.py:24
  312.4 0.8 fusion.27
  313.2 44.6 %fusion.26 = f32[1536]{0:T(1024)S(1)} fusion(f32[1536,2048]{1,0:T(8,128)} %get-tuple-element.135, f32[1536,1024]{1,0:T(8,128)} %get-tuple-element.134, f32[8,2048,1024]{2,1,0:T(8,128)} %get-tuple-element.133, s32[]{:T(128)} %get-tuple-element.122), kind=kOutput, calls=%fused_computation.2.clone.1 | convolution fusion | flops 38660997120 | bytes 27269632 | tf_op jit(solution)/shard_map/while/body/eval_jaxpr/dot_general | solution.py:24
  357.9 0.8 fusion.27
  358.7 44.6 %fusion.26 = f32[1536]{0:T(1024)S(1)} fusion(f32[1536,2048]{1,0:T(8,128)} %get-tuple-element.135, f32[1536,1024]{1,0:T(8,128)} %get-tuple-element.134, f32[8,2048,1024]{2,1,0:T(8,128)} %get-tuple-element.133, s32[]{:T(128)} %get-tuple-element.122), kind=kOutput, calls=%fused_computation.2.clone.1 | convolution fusion | flops 38660997120 | bytes 27269632 | tf_op jit(solution)/shard_map/while/body/eval_jaxpr/dot_general | solution.py:24
  403.4 0.8 fusion.27
  404.3 44.6 %fusion.26 = f32[1536]{0:T(1024)S(1)} fusion(f32[1536,2048]{1,0:T(8,128)} %get-tuple-element.135, f32[1536,1024]{1,0:T(8,128)} %get-tuple-element.134, f32[8,2048,1024]{2,1,0:T(8,128)} %get-tuple-element.133, s32[]{:T(128)} %get-tuple-element.122), kind=kOutput, calls=%fused_computation.2.clone.1 | convolution fusion | flops 38660997120 | bytes 27269632 | tf_op jit(solution)/shard_map/while/body/eval_jaxpr/dot_general | solution.py:24
  448.9 0.8 fusion.27
  449.8 44.6 %fusion.26 = f32[1536]{0:T(1024)S(1)} fusion(f32[1536,2048]{1,0:T(8,128)} %get-tuple-element.135, f32[1536,1024]{1,0:T(8,128)} %get-tuple-element.134, f32[8,2048,1024]{2,1,0:T(8,128)} %get-tuple-element.133, s32[]{:T(128)} %get-tuple-element.122), kind=kOutput, calls=%fused_computation.2.clone.1 | convolution fusion | flops 38660997120 | bytes 27269632 | tf_op jit(solution)/shard_map/while/body/eval_jaxpr/dot_general | solution.py:24
  494.4 0.8 fusion.27
  495.3 38.9 %psum.7 = f32[8,4]{1,0:T(8,128)S(1)} all-reduce(f32[8,4]{1,0:T(8,128)S(1)} %get-tuple-element.37), channel_id=1, replica_groups=mesh['row'=4,'col'=8] {'row','col'}, use_global_device_ids=true, to_apply=%region_3.4 | all-reduce | flops 32 | bytes 256 | tf_op jit(solution)/shard_map/psum | solution.py:31
  534.2 0.0 copy-done.1
  534.2 0.8 convolution_multiply_fusion
  (17 shorter events, 0.3 us)
Async XLA Ops:
  6.5 49.4 %all-gather.3.cloned.1.call-start = ((), (), s32[]{:S(2)}) async-start(), calls=%async_computation | async-start | bytes 3932160 | tf_op jit(solution)/shard_map/all_gather | solution.py:21
  7.3 115.1 %all-gather.5.cloned.1.call-start = ((), (), s32[]{:S(2)}) async-start(), calls=%async_computation.1 | async-start | bytes 7077888 | tf_op jit(solution)/shard_map/all_gather | solution.py:19
  61.1 70.1 %copy-start = (s32[1536]{0:T(1024)S(1)}, s32[1536]{0:T(1024)}, u32[]{:S(2)}) copy-start(s32[1536]{0:T(1024)} %param.12) | copy-start | bytes 18436
  131.2 403.0 %copy-start.1 = (s32[8]{0:T(128)S(1)}, s32[8]{0:T(128)}, u32[]{:S(2)}) copy-start(s32[8]{0:T(128)} %param.13) | copy-start | bytes 100
Sparse Core Ops, SparseCore 0:
  9.2 46.6 all-gather.2
  57.5 64.7 all-gather.4
where the time goes:
time: 542 us
  matrix products  364 us (67%)
  waiting for transfers between devices  110 us (20%)
  blocking collectives  38.9 us (7%)
  other arithmetic  14.8 us (3%)
  between operations  13.4 us (2%)
    dot_general x8, matrix products, one_query(): lax.dot_general(in_wide, query_grad, (((1,), (1,)), ((), ())), precision=...  357 us
    all_gather x1, waiting for transfers between devices, shards(): out_whole = lax.all_gather(out_factors, 'col', axis=0, tiled=True)  61.2 us
    all_gather x1, waiting for transfers between devices, shards(): lax.all_gather(in_factors, 'row', axis=0, tiled=True).astype(jnp.float32)  47.2 us
    psum x1, blocking collectives, shards(): summed = lax.psum(total, ('row', 'col'))  38.9 us
  transfers between devices with their start and end apart: 2, of which 2 were waited for; matrix products, arithmetic and copies ran while one was open for 1% of the time, Pallas kernels for 0%

commit v1 on v0

v1 whole, which is shorter than its diff:
```python
import functools
import math

import jax
import jax.numpy as jnp
from jax import lax
from jax.experimental import pallas as pl
from jax.experimental.pallas import tpu as pltpu
from jax.sharding import PartitionSpec as P

DOUT = 8192
DIN = 8192
SEQ = 4
LEN = 384
SCALE = 1.0 / math.sqrt(DOUT * DIN * LEN)
MESH = pl.DeviceIdType.MESH
MOST = 576
CHUNKS = 8
HALVES = 2
SLOTS = 6
AHEAD = 3
NZ = 4
ORDER = [(0, 0), (1, 0), (2, 0), (3, 0), (0, 1), (1, 1), (2, 1), (3, 1),
         (4, 0), (4, 1), (5, 0), (5, 1), (6, 0), (6, 1), (7, 0), (7, 1)]
RELAY = {2: 2, 3: 3, 4: 4, 6: 5, 9: 6, 12: 7}


def table(n, values):
    got = jnp.int32(values[0])
    for at, value in enumerate(values[1:], 1):
        got = jnp.where(n == at, jnp.int32(value), got)
    return got


def windows(tokens):
    got = []
    for s in range(SEQ):
        first = max(0, tokens - (SEQ - s) * MOST) // 128 * 128
        last = min(tokens, -(-(s + 1) * MOST // 128) * 128)
        got.append((first, last - first))
    return got


def fused(code_ref, ids_ref, out_ref, in_ref, p_ref, res_ref,
          o_buf, o_t, i_buf0, i_buf1, in_w, p_buf, g_buf, wcol, acc_ref, x1, x2,
          p_sem, o_recv, own_sem, sib_sem, fwd_sem, i_recv, i_send,
          x1_recv, x1_send, x2_recv, x2_send):
    nq = p_ref.shape[0]
    rows_n, cols_n = 4, 2 * NZ
    tb, wide = out_ref.shape
    ib, deep = in_ref.shape
    ci = wide // CHUNKS
    cj = deep // HALVES
    row = lax.axis_index("row")
    col = lax.axis_index("col")
    z = col // 2
    core = col % 2
    i_bufs = (i_buf0, i_buf1)

    barrier = pltpu.get_barrier_semaphore()
    for d in range(1, cols_n):
        pl.semaphore_signal(barrier, inc=1, device_id={"col": lax.rem(col + d, cols_n)}, device_id_type=MESH)
    for d in range(1, rows_n):
        pl.semaphore_signal(barrier, inc=1, device_id={"row": lax.rem(row + d, rows_n)}, device_id_type=MESH)

    def p_copy(n):
        k = table(n, [o[0] for o in ORDER])
        h = table(n, [o[1] for o in ORDER])
        slot = lax.rem(n, SLOTS)
        return pltpu.make_async_copy(
            p_ref.at[:, pl.ds(pl.multiple_of(k * ci, ci), ci), pl.ds(pl.multiple_of(h * cj, cj), cj)],
            p_buf.at[slot], p_sem.at[slot])

    for n in range(SLOTS):
        p_copy(jnp.int32(n)).start()
    pl.semaphore_wait(barrier, cols_n - 1 + rows_n - 1)

    def o_rows(src):
        return pl.ds(pl.multiple_of(src * tb, 64), tb)

    def own_copy(k, d):
        dst = lax.rem(z + d, NZ)
        return pltpu.make_async_remote_copy(
            src_ref=out_ref.at[:, pl.ds(pl.multiple_of(k * ci, ci), ci)],
            dst_ref=o_buf.at[k, o_rows(col), :],
            send_sem=own_sem.at[k, d], recv_sem=o_recv.at[k, col],
            device_id={"col": dst * 2 + core}, device_id_type=MESH)

    def direct(d):
        dst = lax.rem(z + d, NZ)
        return jnp.abs(dst - z) < NZ - 1

    def own_sib(k):
        return pltpu.make_async_remote_copy(
            src_ref=out_ref.at[:, pl.ds(pl.multiple_of(k * ci, ci), ci)],
            dst_ref=o_buf.at[k, o_rows(col), :],
            send_sem=sib_sem.at[k, 0], recv_sem=o_recv.at[k, col],
            device_id={"col": z * 2 + 1 - core}, device_id_type=MESH)

    def pass_sib(k, d):
        src = lax.rem(z + d, NZ) * 2 + core
        return pltpu.make_async_remote_copy(
            src_ref=o_buf.at[k, o_rows(src), :], dst_ref=o_buf.at[k, o_rows(src), :],
            send_sem=sib_sem.at[k, d], recv_sem=o_recv.at[k, src],
            device_id={"col": z * 2 + 1 - core}, device_id_type=MESH)

    def ends(d):
        src = lax.rem(z + d, NZ)
        return ((z == NZ - 2) & (src == 0)) | ((z == 1) & (src == NZ - 1))

    def pass_end(k, d):
        zs = lax.rem(z + d, NZ)
        src = zs * 2 + core
        return pltpu.make_async_remote_copy(
            src_ref=o_buf.at[k, o_rows(src), :], dst_ref=o_buf.at[k, o_rows(src), :],
            send_sem=fwd_sem.at[k], recv_sem=o_recv.at[k, src],
            device_id={"col": (NZ - 1 - zs) * 2 + core}, device_id_type=MESH)

    def o_arrived(k, src):
        pltpu.make_async_remote_copy(
            src_ref=o_buf.at[k, o_rows(src), :], dst_ref=o_buf.at[k, o_rows(src), :],
            send_sem=fwd_sem.at[k], recv_sem=o_recv.at[k, src],
            device_id={"col": z * 2 + 1 - core}, device_id_type=MESH).wait_recv()

    def in_copy(h, d):
        return pltpu.make_async_remote_copy(
            src_ref=in_ref.at[:, pl.ds(h * cj, cj)],
            dst_ref=i_bufs[h].at[pl.ds(pl.multiple_of(row * ib, ib), ib), :],
            send_sem=i_send.at[h, d], recv_sem=i_recv.at[h, row],
            device_id={"row": lax.rem(row + d, rows_n)}, device_id_type=MESH)

    def in_arrived(h, d):
        src = lax.rem(row + d, rows_n)
        pltpu.make_async_remote_copy(
            src_ref=in_ref.at[:, pl.ds(h * cj, cj)],
            dst_ref=i_bufs[h].at[pl.ds(pl.multiple_of(src * ib, ib), ib), :],
            send_sem=i_send.at[h, d], recv_sem=i_recv.at[h, src],
            device_id={"row": src}, device_id_type=MESH).wait_recv()

    def send_own(k):
        own_sib(k).start()
        for d in range(1, NZ):
            @pl.when(direct(d))
            def _():
                own_copy(k, d).start()

    def relay(k):
        for d in range(1, NZ):
            src = lax.rem(z + d, NZ) * 2 + core
            o_arrived(k, src)

            @pl.when(ends(d))
            def _():
                pass_end(k, d).start()
            pass_sib(k, d).start()

        @pl.when(k + AHEAD < CHUNKS)
        def _():
            send_own(k + AHEAD)

    for k in range(AHEAD):
        send_own(jnp.int32(k))
        if k < HALVES:
            for d in range(1, rows_n):
                in_copy(k, d).start()

    for k in range(CHUNKS):
        o_buf[k, o_rows(col), :] = out_ref[:, k * ci:(k + 1) * ci]
    for h in range(HALVES):
        i_bufs[h][pl.ds(pl.multiple_of(row * ib, ib), ib), :] = in_ref[:, h * cj:(h + 1) * cj]
    wcol[...] = jnp.transpose(code_ref[...])
    acc_ref[...] = jnp.zeros_like(acc_ref)

    spans = windows(code_ref.shape[1])
    places = [sum(w[1] for w in spans[:s]) for s in range(SEQ)]

    def weigh(h):
        for d in range(1, rows_n):
            in_arrived(h, d)
        for s in range(SEQ):
            first, size = spans[s]
            mine = (wcol[first:first + size, 0:1] == float(s)).astype(jnp.float32)
            in_w[h, places[s]:places[s] + size] = i_bufs[h][first:first + size, :] * mine.astype(jnp.bfloat16)

    relay(jnp.int32(0))
    relay(jnp.int32(1))
    weigh(0)

    def unit(n, carry):
        k = table(n, [o[0] for o in ORDER])
        h = table(n, [o[1] for o in ORDER])
        step = table(n, [RELAY.get(i, 0) for i in range(len(ORDER))])

        @pl.when(step > 0)
        def _():
            relay(step)

        @pl.when(n == 4)
        def _():
            weigh(1)

        @pl.when(h == 0)
        def _():
            for zz in range(NZ):
                o_arrived(k, zz * 2 + 1 - core)
            o_t[k] = jnp.transpose(o_buf[k])

        for s in range(SEQ):
            first, size = spans[s]
            g_buf[s] = jnp.dot(o_t[k, :, first:first + size], in_w[h, places[s]:places[s] + size, :],
                               preferred_element_type=jnp.float32)

        p_copy(n).wait()
        slot = lax.rem(n, SLOTS)

        def strip(r, accs):
            accs = list(accs)
            at = pl.ds(pl.multiple_of(r * 8, 8), 8)
            for lane in range(cj // 128):
                here = pl.ds(lane * 128, 128)
                gs = [g_buf[s, at, here] for s in range(SEQ)]
                for q in range(nq):
                    pq = p_buf[slot, q, at, here]
                    for s in range(SEQ):
                        accs[s * nq + q] = accs[s * nq + q] + pq * gs[s]
            return tuple(accs)

        accs = lax.fori_loop(0, ci // 8, strip, tuple(acc_ref[i] for i in range(SEQ * nq)))
        for i in range(SEQ * nq):
            acc_ref[i] = accs[i]

        @pl.when(n + SLOTS < len(ORDER))
        def _():
            p_copy(n + SLOTS).start()
        return carry

    lax.fori_loop(0, len(ORDER), unit, 0)

    def share(buf, recv, send, name, me, count, value):
        buf[me] = value
        for d in range(1, count):
            pltpu.make_async_remote_copy(
                src_ref=buf.at[me], dst_ref=buf.at[me], send_sem=send.at[d], recv_sem=recv.at[me],
                device_id={name: lax.rem(me + d, count)}, device_id_type=MESH).start()
        for d in range(1, count):
            src = lax.rem(me + d, count)
            pltpu.make_async_remote_copy(
                src_ref=buf.at[src], dst_ref=buf.at[src], send_sem=send.at[d], recv_sem=recv.at[src],
                device_id={name: src}, device_id_type=MESH).wait_recv()
        total = buf[0]
        for i in range(1, count):
            total = total + buf[i]
        return total

    def sent(buf, recv, send, name, me, count):
        for d in range(1, count):
            pltpu.make_async_remote_copy(
                src_ref=buf.at[me], dst_ref=buf.at[me], send_sem=send.at[d], recv_sem=recv.at[me],
                device_id={name: lax.rem(me + d, count)}, device_id_type=MESH).wait_send()

    mine = jnp.sum(acc_ref[...], axis=1)
    total = share(x1, x1_recv, x1_send, "col", col, cols_n, mine)
    total = share(x2, x2_recv, x2_send, "row", row, rows_n, total)
    sums = jnp.sum(total, axis=1, keepdims=True)
    lanes = lax.broadcasted_iota(jnp.int32, (nq, 128), 1)
    raw = jnp.zeros((nq, 128), jnp.float32)
    for s in range(SEQ):
        raw = raw + jnp.where(lanes == s, sums[s * nq:(s + 1) * nq], 0.0)
    picked = jnp.zeros((nq, 128), jnp.float32)
    for q in range(nq):
        picked = picked + jnp.where(ids_ref[...] == q, raw[q:q + 1], 0.0)
    res_ref[...] = picked * SCALE

    def left(k, carry):
        own_sib(k).wait_send()
        for d in range(1, NZ):
            @pl.when(direct(d))
            def _():
                own_copy(k, d).wait_send()

            @pl.when(ends(d))
            def _():
                pass_end(k, d).wait_send()
            pass_sib(k, d).wait_send()
        return carry

    lax.fori_loop(0, CHUNKS, left, 0)
    for h in range(HALVES):
        for d in range(1, rows_n):
            in_copy(h, d).wait_send()
    sent(x1, x1_recv, x1_send, "col", col, cols_n)
    sent(x2, x2_recv, x2_send, "row", row, rows_n)


def local_fused(precond, out_factors, in_factors, token_mask, seq_ids, query_ids):
    nq, wide, deep = precond.shape
    tokens = seq_ids.shape[0]
    code = jnp.where(token_mask == 1, seq_ids, -1).astype(jnp.float32)
    code = jnp.broadcast_to(code[None, :], (8, tokens))
    ids = jnp.broadcast_to(query_ids[:, None], (nq, 128))
    ci, cj = wide // CHUNKS, deep // HALVES
    held = sum(size for _, size in windows(tokens))
    vmem = pl.BlockSpec(memory_space=pltpu.VMEM)
    dma = pltpu.SemaphoreType.DMA
    res = pl.pallas_call(
        fused,
        out_shape=jax.ShapeDtypeStruct((nq, 128), jnp.float32),
        in_specs=[vmem, vmem, vmem, vmem, pl.BlockSpec(memory_space=pl.ANY)],
        out_specs=vmem,
        scratch_shapes=[
            pltpu.VMEM((CHUNKS, tokens, ci), jnp.bfloat16),
            pltpu.VMEM((CHUNKS, ci, tokens), jnp.bfloat16),
            pltpu.VMEM((tokens, cj), jnp.bfloat16),
            pltpu.VMEM((tokens, cj), jnp.bfloat16),
            pltpu.VMEM((HALVES, held, cj), jnp.bfloat16),
            pltpu.VMEM((SLOTS, nq, ci, cj), jnp.float32),
            pltpu.VMEM((SEQ, ci, cj), jnp.float32),
            pltpu.VMEM((tokens, 8), jnp.float32),
            pltpu.VMEM((SEQ * nq, 8, 128), jnp.float32),
            pltpu.VMEM((2 * NZ, SEQ * nq, 128), jnp.float32),
            pltpu.VMEM((4, SEQ * nq, 128), jnp.float32),
            dma((SLOTS,)), dma((CHUNKS, 2 * NZ)), dma((CHUNKS, NZ)), dma((CHUNKS, NZ)),
            dma((CHUNKS,)), dma((HALVES, 4)), dma((HALVES, 4)),
            dma((2 * NZ,)), dma((2 * NZ,)), dma((4,)), dma((4,)),
        ],
        compiler_params=pltpu.CompilerParams(
            collective_id=0, has_side_effects=True, vmem_limit_bytes=60 << 20),
        cost_estimate=pl.CostEstimate(
            flops=2 * wide * deep * (held + SEQ * nq), bytes_accessed=4 * nq * wide * deep, transcendentals=0),
    )(code, ids, out_factors, in_factors, precond)
    return res[:, :SEQ]


def local_plain(precond, out_factors, in_factors, token_mask, seq_ids, query_ids):
    out_whole = lax.all_gather(out_factors, "col", axis=0, tiled=True)
    in_whole = lax.all_gather(in_factors, "row", axis=0, tiled=True)

    def one_sequence(s):
        weight = ((seq_ids == s) & (token_mask == 1)).astype(jnp.bfloat16)
        outer = lax.dot_general(out_whole, in_whole * weight[:, None], (((0,), (0,)), ((), ())),
                                preferred_element_type=jnp.float32)
        return jnp.sum(precond * outer[None], axis=(1, 2))

    total = lax.map(one_sequence, jnp.arange(SEQ, dtype=jnp.int32))
    raw = lax.psum(total, ("row", "col")).T
    select = (query_ids[:, None] == jnp.arange(raw.shape[0], dtype=jnp.int32)[None, :]).astype(jnp.float32)
    return jnp.dot(select, raw, precision=lax.Precision.HIGHEST) * SCALE


def solution(mesh):
    placed = (P(None, "row", "col"), P("col", "row"), P("row", "col"), P(), P(), P())
    small = mesh.shape["row"] == 4 and mesh.shape["col"] == 2 * NZ
    return jax.shard_map(local_fused if small else local_plain, mesh=mesh, in_specs=placed,
                         out_specs=P(), check_vma=False)
```

time: 542 us -> 97.7 us (0.18)
  matrix products: 364 us -> 0 us
  waiting for transfers between devices: 110 us -> 0 us
  Pallas kernels: 0 us -> 93.4 us
  blocking collectives: 38.9 us -> 0 us
  other arithmetic: 14.8 us -> 0.72 us
  between operations: 13.4 us -> 0.01 us
    dot_general x17 -> x0, matrix products: 364 us -> none  [the longest x8 357 us: one_query(): lax.dot_general(in_wide, query_grad, (((1,), (1,)), ((), ())), precision=...]
    all_gather x2 -> x0, waiting for transfers between devices: 108 us -> none  [the longest x1 61.2 us: shards(): out_whole = lax.all_gather(out_factors, 'col', axis=0, tiled=True)]
    pallas_call x0 -> x1, Pallas kernels: none -> 93.4 us  [local_fused(): pl.pallas_call(fused, out_shape=jax.ShapeDtypeStruct((nq, 128), jnp.float...]
    psum x1 -> x0, blocking collectives: 38.9 us -> none  [shards(): summed = lax.psum(total, ('row', 'col'))]
    convert_element_type x3 -> x1, other arithmetic: 14.8 us -> 0.72 us  [local_fused(): code = jnp.where(token_mask == 1, seq_ids, -1).astype(jnp.float32)]
  transfers between devices with their start and end apart: 2 -> 0, of which waited for: 2 -> 0; matrix products, arithmetic and copies ran while one was open for 1% -> 0% of each run, Pallas kernels for 0% -> 0%
where the time goes in v1:
time: 97.7 us; the launch traced here: 97.4 us
  Pallas kernels  93.4 us (96%)
  local copies, waits for them, and re-layouts  3.26 us (3%)
    pallas_call x1, Pallas kernels, local_fused(): pl.pallas_call(fused, out_shape=jax.ShapeDtypeStruct((nq, 128), jnp.float...  93.4 us

profile of v1, /device:TPU:0, one launch (start us, length us, event | category | flops | bytes accessed | tf_op | source)
XLA Modules:
  0.0 97.4 jit_solution(6527003873815450453)
XLA Ops:
  0.0 0.7 select_convert_fusion
  0.7 0.6 broadcast_in_dim.9.code_ref
  1.3 1.3 %broadcast_in_dim.18.ids_ref = s32[8,128]{1,0:T(8,128)} broadcast(s32[8]{0:T(128)} %param.11), dimensions={0} | broadcast | bytes 4128 | tf_op jit(solution)/shard_map/broadcast_in_dim | solution.py:300
  2.7 93.4 %shard_map.64 = f32[8,128]{1,0:T(8,128)} custom-call(f32[8,1536]{1,0:T(8,128)} %broadcast_in_dim.9.code_ref, s32[8,128]{1,0:T(8,128)} %broadcast_in_dim.18.ids_ref, bf16[192,2048]{1,0:T(8,128)(2,1)} %out_ref.1, bf16[384,1024]{1,0:T(8,128)(2,1)} %in_ref.1, f32[8,2048,1024]{2,1,0:T(8,128)} %p_ref.1), custom_call_target="tpu_custom_call" | custom-call | flops 15166603264 | bytes 67108864 | tf_op jit(solution)/shard_map/pallas_call | solution.py:305
  96.0 1.3 %copy.7 = f32[8,4]{0,1:T(4,128)} copy(f32[8,4]{1,0:T(8,128)} %bitcast.1) | data formatting | bytes 256 | tf_op jit(solution)/shard_map/slice | solution.py:331

commit v2 on v1

--- a/solution.py
+++ b/solution.py
@@ -18,7 +18,7 @@
 CHUNKS = 8
 HALVES = 2
 SLOTS = 6
-AHEAD = 3
+AHEAD = 4
 NZ = 4
 ORDER = [(0, 0), (1, 0), (2, 0), (3, 0), (0, 1), (1, 1), (2, 1), (3, 1),
          (4, 0), (4, 1), (5, 0), (5, 1), (6, 0), (6, 1), (7, 0), (7, 1)]
@@ -215,9 +215,9 @@
 
         def strip(r, accs):
             accs = list(accs)
-            at = pl.ds(pl.multiple_of(r * 8, 8), 8)
-            for lane in range(cj // 128):
-                here = pl.ds(lane * 128, 128)
+            for part in range(4 * cj // 128):
+                at = pl.ds(pl.multiple_of(r * 32 + part % 4 * 8, 8), 8)
+                here = pl.ds(part // 4 * 128, 128)
                 gs = [g_buf[s, at, here] for s in range(SEQ)]
                 for q in range(nq):
                     pq = p_buf[slot, q, at, here]
@@ -225,7 +225,7 @@
                         accs[s * nq + q] = accs[s * nq + q] + pq * gs[s]
             return tuple(accs)
 
-        accs = lax.fori_loop(0, ci // 8, strip, tuple(acc_ref[i] for i in range(SEQ * nq)))
+        accs = lax.fori_loop(0, ci // 32, strip, tuple(acc_ref[i] for i in range(SEQ * nq)))
         for i in range(SEQ * nq):
             acc_ref[i] = accs[i]
 

time: 97.7 us -> 95.3 us (0.975); the launches traced: 97.4 us -> 93.8 us
  Pallas kernels: 93.4 us -> 89.8 us
    pallas_call x1, Pallas kernels: 93.4 us -> 89.8 us  [local_fused(): pl.pallas_call(fused, out_shape=jax.ShapeDtypeStruct((nq, 128), jnp.float...]
where the time goes in v2:
time: 95.3 us; the launch traced here: 93.8 us
  Pallas kernels  89.8 us (94%)
  local copies, waits for them, and re-layouts  3.26 us (3%)
    pallas_call x1, Pallas kernels, local_fused(): pl.pallas_call(fused, out_shape=jax.ShapeDtypeStruct((nq, 128), jnp.float...  89.8 us

profile of v2, /device:TPU:0, one launch (start us, length us, event | category | flops | bytes accessed | tf_op | source)
XLA Modules:
  0.0 93.8 jit_solution(6949673252093153419)
XLA Ops:
  0.0 0.7 select_convert_fusion
  0.7 0.6 broadcast_in_dim.9.code_ref
  1.3 1.3 %broadcast_in_dim.18.ids_ref = s32[8,128]{1,0:T(8,128)} broadcast(s32[8]{0:T(128)} %param.11), dimensions={0} | broadcast | bytes 4128 | tf_op jit(solution)/shard_map/broadcast_in_dim | solution.py:300
  2.7 89.8 %shard_map.64 = f32[8,128]{1,0:T(8,128)} custom-call(f32[8,1536]{1,0:T(8,128)} %broadcast_in_dim.9.code_ref, s32[8,128]{1,0:T(8,128)} %broadcast_in_dim.18.ids_ref, bf16[192,2048]{1,0:T(8,128)(2,1)} %out_ref.1, bf16[384,1024]{1,0:T(8,128)(2,1)} %in_ref.1, f32[8,2048,1024]{2,1,0:T(8,128)} %p_ref.1), custom_call_target="tpu_custom_call" | custom-call | flops 15166603264 | bytes 67108864 | tf_op jit(solution)/shard_map/pallas_call | solution.py:305
  92.5 1.3 %copy.7 = f32[8,4]{0,1:T(4,128)} copy(f32[8,4]{1,0:T(8,128)} %bitcast.1) | data formatting | bytes 256 | tf_op jit(solution)/shard_map/slice | solution.py:331
